TPU v7x, 32 devices: a whole 2x2x4 slice. The times are simulated.
32 devices in a mesh: span: 8 (over y, x, core), depth: 4 (over z).
Axes of the slice: x: 2, y: 2, z: 4, core: 2. Of those that a mesh axis runs over, the one named last changes fastest.
Arguments:
- shell_temp: float32 [8, 1024, 256], P('span', 'depth'), may hold values from -6 to 6
- contact_gain: float32 [8, 1024, 256], P('span', 'depth'), may hold values from 0.2 to 2
- die_temp: float32 [48, 256, 1024], P(None, 'span', 'depth'), may hold values from -4 to 4
- diffusivity: float32 [48, 256, 1024], P(None, 'span', 'depth'), may hold values from 0.02 to 0.12
- routes: int32 [8, 1024, 1], P('span', 'depth'), may hold values from 0 to 7; in each aligned block of 256 rows (0 to 255, 256 to 511, ..., all dimensions but the last counted through in order) at most 64 rows name the same one
- tile_rows: int32 [8, 1024], P('span', 'depth'), may hold values from 0 to 31
- closed: int32 [8, 1024], P('span', 'depth'), may hold values 0 or 1
Outputs:
- shell_next: float32 [8, 1024, 256], P('span', 'depth')
- die_next: float32 [48, 256, 1024], P(None, 'span', 'depth')
Inputs may be any that keep to these rules, and one draw needn't show every extreme that they name: `routes`: among the 256 block rows of one device, at most 64 name the same span index, and in some device's rows one span index is named exactly 64 times.
All inputs are finite; a program needn't handle non-finite values. No bound on the sum of `closed` on one device may be relied on, other than what follows from the above.
Results may differ from a plain program's by a relative error of at most 0.00025.
Values sent between devices are 32-bit elements; how exact they have to be, the bound alone decides.
A program may use at most 128 MiB of HBM per device.

v0:
```python
import jax
import jax.numpy as jnp
from jax import lax
from jax.sharding import PartitionSpec as P

STENCIL_WEIGHT = (0.0, 1.0, 0.5, 0.25)
SHELL_RATE = 0.15
SHELL_SINK = 0.5
FACE_GAIN = 0.5


def padded_2(array, sides, width):
    for axis, dim in sides:
        size, length = (lax.axis_size(axis), array.shape[dim])
        up = [(i, (i + 1) % size) for i in range(size - 1)]
        down = [(j, i) for i, j in up]
        last = lax.slice_in_dim(array, length - width, length, axis=dim)
        initial = lax.slice_in_dim(array, 0, width, axis=dim)
        before = lax.ppermute(last, axis, up)
        after = lax.ppermute(initial, axis, down)
        array = jnp.concatenate([before, array, after], axis=dim)
    return array


def stencil_apply(padded):
    depth_count = padded.shape[0]
    rows_inner = padded.shape[1] - 2
    cols_inner = padded.shape[2] - 2
    framed = jnp.pad(padded, ((1, 1), (0, 0), (0, 0)))
    summed = -14.0 * padded[:, 1:-1, 1:-1]
    for step_z in range(3):
        for step_x in range(3):
            for step_y in range(3):
                reach_count = abs(step_z - 1) + abs(step_x - 1) + abs(step_y - 1)
                if reach_count > 0:
                    summed = (
                        summed
                        + STENCIL_WEIGHT[reach_count]
                        * framed[
                            step_z : step_z + depth_count,
                            step_x : step_x + rows_inner,
                            step_y : step_y + cols_inner,
                        ]
                    )
    return summed


def deposit(tile_codes, flux_rows, row_count):
    select = (jnp.arange(row_count, dtype=jnp.int32)[:, None] == tile_codes[None, :]).astype(
        jnp.float32
    )
    return jnp.dot(
        select, flux_rows, precision=lax.Precision.HIGHEST, preferred_element_type=jnp.float32
    )


def local(shell_temp, contact_gain, die_temp, diffusivity, routes, tile_rows, closed):
    shells = shell_temp[0]
    shell_gain = contact_gain[0]
    block_count, block_width = shells.shape
    span_count = lax.axis_size("span")
    capacity = 2 * block_count // span_count
    slot_count = span_count * capacity
    rimmed = padded_2(shells, (("depth", 0),), 1)
    framed = jnp.pad(rimmed, ((0, 0), (1, 1)))
    laplace = (
        framed[2:, 1:-1] + framed[:-2, 1:-1] + framed[1:-1, 2:] + framed[1:-1, :-2] - 4.0 * shells
    )
    target = routes[0, :, 0]
    span_ids = jnp.arange(span_count, dtype=jnp.int32)
    member = (target[:, None] == span_ids[None, :]).astype(jnp.int32)
    earlier = jnp.cumsum(member, axis=0) - member
    slot_index = jnp.sum(earlier * member, axis=1)
    position = target * capacity + slot_index
    tile_code = jnp.where(closed[0] > 0, tile_rows[0], -1)
    face_rows = die_temp[0]
    row_count = face_rows.shape[0]
    empty_slots = jnp.zeros((slot_count, block_width), jnp.float32)
    send_temp = empty_slots.at[position].set(shells)
    send_gain = empty_slots.at[position].set(shell_gain)
    send_code = (
        jnp.full((slot_count,), -1.0, jnp.float32).at[position].set(tile_code.astype(jnp.float32))
    )
    got_temp, got_gain, got_code = (
        lax.all_to_all(send_temp, "span", split_axis=0, concat_axis=0, tiled=True),
        lax.all_to_all(send_gain, "span", split_axis=0, concat_axis=0, tiled=True),
        lax.all_to_all(send_code, "span", split_axis=0, concat_axis=0, tiled=True),
    )
    got_tile = got_code.astype(jnp.int32)
    slot_live = (got_tile >= 0).astype(jnp.float32)
    face_values = face_rows[jnp.maximum(got_tile, 0)]
    flux_slots = got_gain * (got_temp - face_values) * slot_live[:, None]
    heat_in = deposit(got_tile, flux_slots, row_count)
    flux_back = lax.all_to_all(flux_slots, "span", split_axis=0, concat_axis=0, tiled=True)
    flux_mine = flux_back[position]
    shell_next = shells + SHELL_RATE * laplace - SHELL_SINK * flux_mine
    heated_face = face_rows + FACE_GAIN * heat_in
    heated = jnp.concatenate([heated_face[None], die_temp[1:]], axis=0)
    field = heated
    for sweep_index in range(2):
        padded = padded_2(field, (("span", 1), ("depth", 2)), 1)
        field = field + diffusivity * stencil_apply(padded)
    return (shell_next[None], field)


def solution(mesh):
    placed = (
        P("span", "depth", None),
        P("span", "depth", None),
        P(None, "span", "depth"),
        P(None, "span", "depth"),
        P("span", "depth", None),
        P("span", "depth"),
        P("span", "depth"),
    )
    return jax.shard_map(
        local,
        mesh=mesh,
        in_specs=placed,
        out_specs=(P("span", "depth", None), P(None, "span", "depth")),
        check_vma=False,
    )
```

profile of v0, /device:TPU:1, one launch (start us, length us, event | category | flops | bytes accessed | tf_op | source)
XLA Modules:
  0.0 137.0 jit_solution(14575713565033971148)
XLA Ops:
  0.6 0.0 copy-start
  0.6 0.7 fusion.79
  1.4 0.6 reduce-window.6
  1.9 0.2 slice_reduce_fusion
  2.2 0.8 fusion.78
  3.0 0.7 compare_select_fusion
  3.7 0.7 fusion.80
  4.4 1.4 %scatter_custom_fusion.2 = f32[512]{0:T(512)S(1)} fusion(s32[256]{0:T(256)S(1)} %bitcast.58, f32[256]{0:T(256)S(1)} %bitcast.63, f32[]{:T(128)} %constant.5.clone.1), kind=kCustom, calls=%fused_computation.180 | custom fusion | bytes 2052 | tf_op jit(solution)/shard_map/scatter | solution.py:82
  5.8 0.7 all_to_all.32
  6.4 5.2 %all-to-all-start.2 = ((f32[8,64,1]{1,2,0:T(1,128)}), f32[8,64,1]{1,2,0:T(1,128)S(1)}, u32[]{:S(2)}, u32[]{:S(2)}) async-start(f32[8,64,1]{1,2,0:T(1,128)} %all_to_all.32), calls=%async_computation.2 | async-start | bytes 8192 | tf_op jit(solution)/shard_map/all_to_all | solution.py:87
  11.7 2.6 %scatter_custom_fusion.1 = f32[512,256]{1,0:T(8,128)} fusion(s32[256]{0:T(256)S(1)} %bitcast.59, f32[]{:T(128)} %constant.11.clone.1, f32[1,256,256]{2,1,0:T(8,128)} %param.7), kind=kCustom, calls=%fused_computation.157 | custom fusion | bytes 786436 | tf_op jit(solution)/shard_map/scatter | solution.py:79
  14.3 1.3 all-to-all-done.2
  15.5 4.1 %all-to-all-start.1 = ((f32[8,64,256]{2,1,0:T(8,128)}), f32[8,64,256]{2,1,0:T(8,128)S(1)}, u32[]{:S(2)}, u32[]{:S(2)}) async-start(f32[8,64,256]{2,1,0:T(8,128)} %bitcast.12), calls=%async_computation.1 | async-start | bytes 1048576 | tf_op jit(solution)/shard_map/all_to_all | solution.py:85
  19.6 1.3 slice_bitcast_fusion.1
  20.9 3.2 %collective-permute-start.1 = (f32[1,256]{1,0:T(1,128)}, f32[1,256]{1,0:T(1,128)S(1)}, u32[]{:S(2)}, u32[]{:S(2)}) collective-permute-start(f32[1,256]{1,0:T(1,128)} %get-tuple-element.20), channel_id=1, source_target_pairs={{0,1},{1,2},{2,3},{4,5},{5,6},{6,7},{8,9},{9,10},{10,11},{12,13},{... | collective-permute-start | bytes 3080 | tf_op jit(solution)/shard_map/ppermute | solution.py:19
  24.1 1.3 collective-permute-start
  25.5 2.2 %scatter_custom_fusion = f32[512,256]{1,0:T(8,128)} fusion(s32[256]{0:T(256)S(1)} %bitcast.60, f32[1,256,256]{2,1,0:T(8,128)S(1)} %copy-done, f32[]{:T(128)} %constant.11.clone.1), kind=kCustom, calls=%fused_computation.155 | custom fusion | bytes 786436 | tf_op jit(solution)/shard_map/scatter | solution.py:80
  27.7 5.8 %all-to-all-start = ((f32[8,64,256]{2,1,0:T(8,128)}), f32[8,64,256]{2,1,0:T(8,128)}, u32[]{:S(2)}, u32[]{:S(2)}) async-start(f32[8,64,256]{2,1,0:T(8,128)} %bitcast.11), calls=%async_computation | async-start | bytes 1048576 | tf_op jit(solution)/shard_map/all_to_all | solution.py:86
  33.5 0.8 slice_bitcast_fusion
  34.2 1.5 %slice.267 = f32[47,32,256]{2,1,0:T(8,128)S(1)} slice(f32[48,32,256]{2,1,0:T(8,128)} %param.9), slice={[1:48], [0:32], [0:256]} | slice | bytes 3080192 | tf_op jit(solution)/shard_map/slice | solution.py:98
  35.8 0.1 convert_element_type.62
  35.8 0.1 reshape.107
  35.9 1.6 %gather_fusion = f32[512,256]{1,0:T(8,128)S(1)} fusion(f32[32,256]{1,0:T(8,128)S(1)} %slice_bitcast_fusion, s32[1024]{0:T(1024)S(1)} %pad_clamp_fusion.1), kind=kCustom, calls=%fused_computation | custom fusion | bytes 1050624 | tf_op jit(solution)/shard_map/gather | solution.py:91
  37.5 2.8 %all-to-all-done = f32[8,64,256]{2,1,0:T(8,128)} async-done(((f32[8,64,256]{2,1,0:T(8,128)}), f32[8,64,256]{2,1,0:T(8,128)}, u32[]{:S(2)}, u32[]{:S(2)}) %all-to-all-start) | async-done | bytes 524320 | tf_op jit(solution)/shard_map/all_to_all | solution.py:86
  40.3 1.2 fusion.63
  41.6 1.1 fusion.61
  42.6 0.2 pad_maximum_fusion.9
  42.8 0.9 copy.52
  43.7 0.0 copy-start.7
  43.7 1.1 copy-done.7
  44.9 5.1 %collective-permute-start.2 = (f32[48,1,256]{2,0,1:T(8,128)S(1)}, f32[48,1,256]{2,0,1:T(8,128)S(1)}, u32[]{:S(2)}, u32[]{:S(2)}) collective-permute-start(f32[48,1,256]{2,0,1:T(8,128)S(1)} %get-tuple-element.18), channel_id=1, source_target_pairs={{0,4},{4,8},{8,12},{12,16},{16,20},{20,24},{24,28},{1,5},{5,9},{9,... | collective-permute-start | bytes 147464 | tf_op jit(solution)/shard_map/ppermute | solution.py:19
  50.0 1.9 %collective-permute-start.3 = (f32[48,1,256]{2,0,1:T(8,128)S(1)}, f32[48,1,256]{2,0,1:T(8,128)S(1)}, u32[]{:S(2)}, u32[]{:S(2)}) collective-permute-start(f32[48,1,256]{2,0,1:T(8,128)S(1)} %get-tuple-element.19), channel_id=1, source_target_pairs={{4,0},{8,4},{12,8},{16,12},{20,16},{24,20},{28,24},{5,1},{9,5},{13... | collective-permute-start | bytes 147464 | tf_op jit(solution)/shard_map/ppermute | solution.py:20
  51.9 4.4 %copy.40 = f32[48,32,256]{0,1,2:T(8,128)} copy(f32[48,32,256]{2,1,0:T(8,128)S(1)} %pad_maximum_fusion.9) | data formatting | bytes 3145728 | tf_op jit(solution)/shard_map/concatenate | solution.py:98
  56.4 0.1 copy.41
  56.5 0.1 copy.39
  56.6 3.2 %pad_maximum_fusion = f32[48,34,256]{0,1,2:T(8,128)S(1)} fusion(f32[48,1,256]{0,1,2:T(1,128)S(1)} %copy.41, f32[48,32,256]{0,1,2:T(8,128)} %copy.40, f32[48,1,256]{0,1,2:T(1,128)S(1)} %copy.39), kind=kLoop, calls=%fused_computation.5 | loop fusion | flops 835584 | bytes 3342336 | tf_op jit(solution)/shard_map/concatenate | solution.py:21
  59.8 2.3 %copy-done.3 = f32[48,34,256]{0,1,2:T(8,128)} copy-done((f32[48,34,256]{0,1,2:T(8,128)}, f32[48,34,256]{0,1,2:T(8,128)S(1)}, u32[]{:S(2)}) %copy-start.3) | copy-done | bytes 1671192
  62.1 3.2 %collective-permute-start.4 = (f32[48,34,1]{0,1,2:T(8,128)S(1)}, f32[48,34,1]{0,1,2:T(8,128)S(1)}, u32[]{:S(2)}, u32[]{:S(2)}) collective-permute-start(f32[48,34,1]{0,1,2:T(8,128)S(1)} %get-tuple-element.10), channel_id=1, source_target_pairs={{0,1},{1,2},{2,3},{4,5},{5,6},{6,7},{8,9},{9,10},{10,11},{12,13},{... | collective-permute-start | bytes 19592 | tf_op jit(solution)/shard_map/ppermute | solution.py:19
  65.3 1.5 %collective-permute-start.5 = (f32[48,34,1]{0,1,2:T(8,128)S(1)}, f32[48,34,1]{0,1,2:T(8,128)S(1)}, u32[]{:S(2)}, u32[]{:S(2)}) collective-permute-start(f32[48,34,1]{0,1,2:T(8,128)S(1)} %get-tuple-element.11), channel_id=1, source_target_pairs={{1,0},{2,1},{3,2},{5,4},{6,5},{7,6},{9,8},{10,9},{11,10},{13,12},{... | collective-permute-start | bytes 19592 | tf_op jit(solution)/shard_map/ppermute | solution.py:20
  66.8 1.0 select_maximum_fusion.6
  67.8 4.9 %copy.43 = f32[48,34,256]{2,0,1:T(8,128)S(1)} copy(f32[48,34,256]{0,1,2:T(8,128)} %copy-done.3) | data formatting | bytes 3342336 | tf_op jit(solution)/shard_map/concatenate | solution.py:21
  72.7 0.3 copy.44
  73.1 1.3 copy.42
  74.4 2.4 %select_maximum_fusion.4 = f32[50,34,258]{2,0,1:T(8,128)S(1)} fusion(f32[48,34,1]{2,0,1:T(8,128)S(1)} %copy.44, f32[48,34,256]{2,0,1:T(8,128)S(1)} %copy.43, f32[48,34,1]{2,0,1:T(8,128)} %copy.42), kind=kLoop, calls=%fused_computation.16 | loop fusion | flops 3508800 | bytes 3438624 | tf_op jit(solution)/shard_map/concatenate | solution.py:21
  76.8 9.6 %fusion.16 = f32[48,32,256]{2,0,1:T(8,128)S(1)} fusion(f32[48,32,256]{2,0,1:T(8,128)S(1)} %copy-done.8, f32[48,34,256]{2,0,1:T(8,128)S(1)} %copy.43, f32[48,34,1]{2,0,1:T(8,128)S(1)} %copy.44, f32[48,34,1]{2,0,1:T(8,128)S(1)} %copy-done.6, f32[50,34,258]{2,0,1:T(8,128)S(1)} %select_maximum_fusion.4, f32[48,1,256]{2,0,1:T(8,128)S(1)} %collective-permute-done.3, ...), kind=kLoop, calls=%fused_computation.41 | loop fusion | flops 22413312 | bytes 34812672 | tf_op jit(solution)/shard_map/add | solution.py:102
  86.4 3.9 %collective-permute-start.6 = (f32[48,1,256]{2,0,1:T(8,128)S(1)}, f32[48,1,256]{2,0,1:T(8,128)S(1)}, u32[]{:S(2)}, u32[]{:S(2)}) collective-permute-start(f32[48,1,256]{2,0,1:T(8,128)S(1)} %get-tuple-element.16), channel_id=1, source_target_pairs={{0,4},{4,8},{8,12},{12,16},{16,20},{20,24},{24,28},{1,5},{5,9},{9,... | collective-permute-start | bytes 147464 | tf_op jit(solution)/shard_map/ppermute | solution.py:19
  90.4 1.9 %collective-permute-start.7 = (f32[48,1,256]{2,0,1:T(8,128)S(1)}, f32[48,1,256]{2,0,1:T(8,128)S(1)}, u32[]{:S(2)}, u32[]{:S(2)}) collective-permute-start(f32[48,1,256]{2,0,1:T(8,128)S(1)} %get-tuple-element.17), channel_id=1, source_target_pairs={{4,0},{8,4},{12,8},{16,12},{20,16},{24,20},{28,24},{5,1},{9,5},{13... | collective-permute-start | bytes 147464 | tf_op jit(solution)/shard_map/ppermute | solution.py:20
  92.3 3.5 %collective-permute-done.7 = f32[48,1,256]{2,0,1:T(8,128)S(1)} collective-permute-done((f32[48,1,256]{2,0,1:T(8,128)S(1)}, f32[48,1,256]{2,0,1:T(8,128)S(1)}, u32[]{:S(2)}, u32[]{:S(2)}) %collective-permute-start.7) | collective-permute-done | bytes 49184 | tf_op jit(solution)/shard_map/ppermute | solution.py:20
  95.8 0.1 pad_maximum_fusion.2
  95.9 0.3 fusion.85
  96.2 0.4 copy.61
  96.6 0.4 copy.62
  97.0 1.3 collective-permute-start.9
  98.3 4.9 %collective-permute-start.8 = (f32[48,34,1]{0,1,2:T(8,128)S(1)}, f32[48,34,1]{0,1,2:T(8,128)S(1)}, u32[]{:S(2)}, u32[]{:S(2)}) collective-permute-start(f32[48,34,1]{0,1,2:T(8,128)S(1)} %copy.61), channel_id=1, source_target_pairs={{0,1},{1,2},{2,3},{4,5},{5,6},{6,7},{8,9},{9,10},{10,11},{12,13},{... | collective-permute-start | bytes 19592 | tf_op jit(solution)/shard_map/ppermute | solution.py:19
  103.2 2.0 %multiply_multiply_fusion = f32[8,64,256]{2,1,0:T(8,128)} fusion(f32[8,64,256]{2,1,0:T(8,128)} %all-to-all-done, f32[8,64,256]{2,1,0:T(8,128)S(1)} %copy-done.13, f32[8,64,256]{2,1,0:T(8,128)S(1)} %bitcast.52, f32[8,64]{1,0:T(8,128)S(1)} %bitcast.55), kind=kLoop, calls=%fused_computation.141 | loop fusion | flops 393216 | bytes 2099200 | tf_op jit(solution)/shard_map/mul | solution.py:92
  105.2 4.6 %all-to-all-start.3 = ((f32[8,64,256]{2,1,0:T(8,128)}), f32[8,64,256]{2,1,0:T(8,128)}, u32[]{:S(2)}, u32[]{:S(2)}) async-start(f32[8,64,256]{2,1,0:T(8,128)} %multiply_multiply_fusion), calls=%async_computation.3 | async-start | bytes 1048576 | tf_op jit(solution)/shard_map/all_to_all | solution.py:94
  109.8 1.3 copy.55
  111.1 1.3 copy.56
  112.4 3.2 %select_maximum_fusion = f32[50,34,258]{2,0,1:T(8,128)S(1)} fusion(f32[48,34,1]{2,0,1:T(8,128)} %copy.56, f32[48,34,1]{2,0,1:T(8,128)} %copy.55, f32[48,1,256]{2,0,1:T(8,128)S(1)} %collective-permute-done.7, f32[48,32,256]{2,0,1:T(8,128)} %copy-done.1, f32[48,1,256]{2,0,1:T(8,128)S(1)} %collective-permute-done.6), kind=kLoop, calls=%fused_computation.12 | loop fusion | flops 5263200 | bytes 3438624 | tf_op jit(solution)/shard_map/concatenate | solution.py:21
  115.6 3.0 %maximum_maximum_fusion = (f32[48,34,257]{2,0,1:T(8,128)}, f32[48,34,257]{2,0,1:T(8,128)}) fusion(f32[48,1,256]{2,0,1:T(8,128)S(1)} %collective-permute-done.7, f32[48,32,256]{2,0,1:T(8,128)S(1)} %copy-done.2, f32[48,1,256]{2,0,1:T(8,128)S(1)} %collective-permute-done.6, f32[48,34,1]{2,0,1:T(8,128)S(1)} %copy-done.4, f32[48,34,1]{2,0,1:T(8,128)S(1)} %copy-done.5), kind=kLoop, calls=%fused_computation.23 | loop fusion | flops 2516544 | bytes 5039616 | tf_op jit(solution)/shard_map/concatenate | solution.py:21
  118.7 11.8 %fusion.28 = f32[48,32,256]{2,0,1:T(8,128)} fusion(f32[48,32,256]{2,0,1:T(8,128)} %copy-done.1, f32[50,34,258]{2,0,1:T(8,128)S(1)} %select_maximum_fusion, f32[48,34,257]{2,0,1:T(8,128)} %get-tuple-element.13, f32[48,1,256]{2,0,1:T(8,128)S(1)} %collective-permute-done.7, f32[48,34,257]{2,0,1:T(8,128)} %get-tuple-element.12, ...), kind=kLoop, calls=%fused_computation.54 | loop fusion | flops 20054016 | bytes 42565632 | tf_op jit(solution)/shard_map/add | solution.py:102
  130.5 3.5 %copy.60 = f32[48,32,256]{2,1,0:T(8,128)} copy(f32[48,32,256]{2,0,1:T(8,128)} %fusion.28) | data formatting | bytes 3145728
  134.0 2.1 %gather_fusion.1 = f32[256,256]{1,0:T(8,128)S(1)} fusion(f32[512,256]{1,0:T(8,128)} %bitcast.17, s32[1024]{0:T(1024)S(1)} %pad_clamp_fusion), kind=kCustom, calls=%fused_computation.1 | custom fusion | bytes 525312 | tf_op jit(solution)/shard_map/gather | solution.py:95
  136.1 0.9 fusion.69
  (57 shorter events, 0.2 us)
Async XLA Ops:
  0.6 24.8 %copy-start = (f32[1,256,256]{2,1,0:T(8,128)S(1)}, f32[1,256,256]{2,1,0:T(8,128)}, u32[]{:S(2)}) copy-start(f32[1,256,256]{2,1,0:T(8,128)} %param.8) | copy-start | bytes 786436
  6.4 9.1 %all-to-all-start.2 = ((f32[8,64,1]{1,2,0:T(1,128)}), f32[8,64,1]{1,2,0:T(1,128)S(1)}, u32[]{:S(2)}, u32[]{:S(2)}) async-start(f32[8,64,1]{1,2,0:T(1,128)} %all_to_all.32), calls=%async_computation.2 | async-start | bytes 8192 | tf_op jit(solution)/shard_map/all_to_all | solution.py:87
  15.5 12.1 %all-to-all-start.1 = ((f32[8,64,256]{2,1,0:T(8,128)}), f32[8,64,256]{2,1,0:T(8,128)S(1)}, u32[]{:S(2)}, u32[]{:S(2)}) async-start(f32[8,64,256]{2,1,0:T(8,128)} %bitcast.12), calls=%async_computation.1 | async-start | bytes 1048576 | tf_op jit(solution)/shard_map/all_to_all | solution.py:85
  20.9 45.8 %collective-permute-start.1 = (f32[1,256]{1,0:T(1,128)}, f32[1,256]{1,0:T(1,128)S(1)}, u32[]{:S(2)}, u32[]{:S(2)}) collective-permute-start(f32[1,256]{1,0:T(1,128)} %get-tuple-element.20), channel_id=1, source_target_pairs={{0,1},{1,2},{2,3},{4,5},{5,6},{6,7},{8,9},{9,10},{10,11},{12,13},{... | collective-permute-start | bytes 3080 | tf_op jit(solution)/shard_map/ppermute | solution.py:19
  24.1 42.6 %collective-permute-start = (f32[1,256]{1,0:T(1,128)S(1)}, f32[1,256]{1,0:T(1,128)S(1)}, u32[]{:S(2)}, u32[]{:S(2)}) collective-permute-start(f32[1,256]{1,0:T(1,128)S(1)} %get-tuple-element.21), channel_id=1, source_target_pairs={{1,0},{2,1},{3,2},{5,4},{6,5},{7,6},{9,8},{10,9},{11,10},{13,12},{... | collective-permute-start | bytes 3080 | tf_op jit(solution)/shard_map/ppermute | solution.py:20
  27.7 12.7 %copy-start.12 = (f32[8,64,256]{2,1,0:T(8,128)}, f32[8,64,256]{2,1,0:T(8,128)S(1)}, u32[]{:S(2)}) copy-start(f32[8,64,256]{2,1,0:T(8,128)S(1)} %all-to-all-done.1) | copy-start | bytes 1572868
  27.7 12.6 %all-to-all-start = ((f32[8,64,256]{2,1,0:T(8,128)}), f32[8,64,256]{2,1,0:T(8,128)}, u32[]{:S(2)}, u32[]{:S(2)}) async-start(f32[8,64,256]{2,1,0:T(8,128)} %bitcast.11), calls=%async_computation | async-start | bytes 1048576 | tf_op jit(solution)/shard_map/all_to_all | solution.py:86
  37.5 4.1 %copy-start.10 = (f32[512,256]{1,0:T(8,128)}, f32[512,256]{1,0:T(8,128)S(1)}, u32[]{:S(2)}) copy-start(f32[512,256]{1,0:T(8,128)S(1)} %gather_fusion) | copy-start | bytes 1572868
  43.7 1.1 copy-start.7
  44.9 11.6 %collective-permute-start.2 = (f32[48,1,256]{2,0,1:T(8,128)S(1)}, f32[48,1,256]{2,0,1:T(8,128)S(1)}, u32[]{:S(2)}, u32[]{:S(2)}) collective-permute-start(f32[48,1,256]{2,0,1:T(8,128)S(1)} %get-tuple-element.18), channel_id=1, source_target_pairs={{0,4},{4,8},{8,12},{12,16},{16,20},{20,24},{24,28},{1,5},{5,9},{9,... | collective-permute-start | bytes 147464 | tf_op jit(solution)/shard_map/ppermute | solution.py:19
  50.0 6.4 %collective-permute-start.3 = (f32[48,1,256]{2,0,1:T(8,128)S(1)}, f32[48,1,256]{2,0,1:T(8,128)S(1)}, u32[]{:S(2)}, u32[]{:S(2)}) collective-permute-start(f32[48,1,256]{2,0,1:T(8,128)S(1)} %get-tuple-element.19), channel_id=1, source_target_pairs={{4,0},{8,4},{12,8},{16,12},{20,16},{24,20},{28,24},{5,1},{9,5},{13... | collective-permute-start | bytes 147464 | tf_op jit(solution)/shard_map/ppermute | solution.py:20
  56.6 10.2 %copy-start.14 = (f32[1,256,256]{2,1,0:T(8,128)S(1)}, f32[1,256,256]{2,1,0:T(8,128)}, u32[]{:S(2)}) copy-start(f32[1,256,256]{2,1,0:T(8,128)} %param.7) | copy-start | bytes 786436
  59.7 2.3 %copy-start.3 = (f32[48,34,256]{0,1,2:T(8,128)}, f32[48,34,256]{0,1,2:T(8,128)S(1)}, u32[]{:S(2)}) copy-start(f32[48,34,256]{0,1,2:T(8,128)S(1)} %pad_maximum_fusion) | copy-start | bytes 5013508
  62.1 11.0 %collective-permute-start.4 = (f32[48,34,1]{0,1,2:T(8,128)S(1)}, f32[48,34,1]{0,1,2:T(8,128)S(1)}, u32[]{:S(2)}, u32[]{:S(2)}) collective-permute-start(f32[48,34,1]{0,1,2:T(8,128)S(1)} %get-tuple-element.10), channel_id=1, source_target_pairs={{0,1},{1,2},{2,3},{4,5},{5,6},{6,7},{8,9},{9,10},{10,11},{12,13},{... | collective-permute-start | bytes 19592 | tf_op jit(solution)/shard_map/ppermute | solution.py:19
  65.3 7.5 %collective-permute-start.5 = (f32[48,34,1]{0,1,2:T(8,128)S(1)}, f32[48,34,1]{0,1,2:T(8,128)S(1)}, u32[]{:S(2)}, u32[]{:S(2)}) collective-permute-start(f32[48,34,1]{0,1,2:T(8,128)S(1)} %get-tuple-element.11), channel_id=1, source_target_pairs={{1,0},{2,1},{3,2},{5,4},{6,5},{7,6},{9,8},{10,9},{11,10},{13,12},{... | collective-permute-start | bytes 19592 | tf_op jit(solution)/shard_map/ppermute | solution.py:20
  66.8 5.9 %copy-start.16 = (f32[1,256]{1,0:T(1,128)}, f32[1,256]{1,0:T(1,128)S(1)}, u32[]{:S(2)}) copy-start(f32[1,256]{1,0:T(1,128)S(1)} %collective-permute-done.1) | copy-start | bytes 3076
  66.8 5.9 %copy-start.18 = (f32[1,256]{1,0:T(1,128)}, f32[1,256]{1,0:T(1,128)S(1)}, u32[]{:S(2)}) copy-start(f32[1,256]{1,0:T(1,128)S(1)} %collective-permute-done) | copy-start | bytes 3076
  74.3 2.5 %copy-start.6 = (f32[48,34,1]{2,0,1:T(8,128)S(1)}, f32[48,34,1]{2,0,1:T(8,128)}, u32[]{:S(2)}) copy-start(f32[48,34,1]{2,0,1:T(8,128)} %copy.42) | copy-start | bytes 19588
  74.3 2.5 %copy-start.8 = (f32[48,32,256]{2,0,1:T(8,128)S(1)}, f32[48,32,256]{2,0,1:T(8,128)}, u32[]{:S(2)}) copy-start(f32[48,32,256]{2,0,1:T(8,128)} %copy-done.7) | copy-start | bytes 4718596
  74.4 2.5 %copy-start.9 = (f32[48,32,256]{2,1,0:T(8,128)S(1)}, f32[48,32,256]{2,1,0:T(8,128)}, u32[]{:S(2)}) copy-start(f32[48,32,256]{2,1,0:T(8,128)} %param.10) | copy-start | bytes 4718596
  86.4 9.5 %copy-start.1 = (f32[48,32,256]{2,0,1:T(8,128)}, f32[48,32,256]{2,0,1:T(8,128)S(1)}, u32[]{:S(2)}) copy-start(f32[48,32,256]{2,0,1:T(8,128)S(1)} %fusion.16) | copy-start | bytes 4718596
  86.4 5.9 %collective-permute-start.6 = (f32[48,1,256]{2,0,1:T(8,128)S(1)}, f32[48,1,256]{2,0,1:T(8,128)S(1)}, u32[]{:S(2)}, u32[]{:S(2)}) collective-permute-start(f32[48,1,256]{2,0,1:T(8,128)S(1)} %get-tuple-element.16), channel_id=1, source_target_pairs={{0,4},{4,8},{8,12},{12,16},{16,20},{20,24},{24,28},{1,5},{5,9},{9,... | collective-permute-start | bytes 147464 | tf_op jit(solution)/shard_map/ppermute | solution.py:19
  90.4 5.4 %collective-permute-start.7 = (f32[48,1,256]{2,0,1:T(8,128)S(1)}, f32[48,1,256]{2,0,1:T(8,128)S(1)}, u32[]{:S(2)}, u32[]{:S(2)}) collective-permute-start(f32[48,1,256]{2,0,1:T(8,128)S(1)} %get-tuple-element.17), channel_id=1, source_target_pairs={{4,0},{8,4},{12,8},{16,12},{20,16},{24,20},{28,24},{5,1},{9,5},{13... | collective-permute-start | bytes 147464 | tf_op jit(solution)/shard_map/ppermute | solution.py:20
  96.2 7.0 %copy-start.11 = (f32[512,256]{1,0:T(8,128)S(1)}, f32[512,256]{1,0:T(8,128)}, u32[]{:S(2)}) copy-start(f32[512,256]{1,0:T(8,128)} %copy-done.10) | copy-start | bytes 1572868
  96.2 7.0 %copy-start.13 = (f32[8,64,256]{2,1,0:T(8,128)S(1)}, f32[8,64,256]{2,1,0:T(8,128)}, u32[]{:S(2)}) copy-start(f32[8,64,256]{2,1,0:T(8,128)} %copy-done.12) | copy-start | bytes 1572868
  97.0 14.2 %collective-permute-start.9 = (f32[48,34,1]{0,1,2:T(8,128)S(1)}, f32[48,34,1]{0,1,2:T(8,128)S(1)}, u32[]{:S(2)}, u32[]{:S(2)}) collective-permute-start(f32[48,34,1]{0,1,2:T(8,128)S(1)} %copy.62), channel_id=1, source_target_pairs={{1,0},{2,1},{3,2},{5,4},{6,5},{7,6},{9,8},{10,9},{11,10},{13,12},{... | collective-permute-start | bytes 19592 | tf_op jit(solution)/shard_map/ppermute | solution.py:20
  98.3 11.5 %collective-permute-start.8 = (f32[48,34,1]{0,1,2:T(8,128)S(1)}, f32[48,34,1]{0,1,2:T(8,128)S(1)}, u32[]{:S(2)}, u32[]{:S(2)}) collective-permute-start(f32[48,34,1]{0,1,2:T(8,128)S(1)} %copy.61), channel_id=1, source_target_pairs={{0,1},{1,2},{2,3},{4,5},{5,6},{6,7},{8,9},{9,10},{10,11},{12,13},{... | collective-permute-start | bytes 19592 | tf_op jit(solution)/shard_map/ppermute | solution.py:19
  105.2 28.8 %all-to-all-start.3 = ((f32[8,64,256]{2,1,0:T(8,128)}), f32[8,64,256]{2,1,0:T(8,128)}, u32[]{:S(2)}, u32[]{:S(2)}) async-start(f32[8,64,256]{2,1,0:T(8,128)} %multiply_multiply_fusion), calls=%async_computation.3 | async-start | bytes 1048576 | tf_op jit(solution)/shard_map/all_to_all | solution.py:94
  112.4 3.2 %copy-start.2 = (f32[48,32,256]{2,0,1:T(8,128)S(1)}, f32[48,32,256]{2,0,1:T(8,128)}, u32[]{:S(2)}) copy-start(f32[48,32,256]{2,0,1:T(8,128)} %copy-done.1) | copy-start | bytes 4718596
  112.4 3.2 %copy-start.4 = (f32[48,34,1]{2,0,1:T(8,128)S(1)}, f32[48,34,1]{2,0,1:T(8,128)}, u32[]{:S(2)}) copy-start(f32[48,34,1]{2,0,1:T(8,128)} %copy.55) | copy-start | bytes 19588
  112.4 3.2 %copy-start.5 = (f32[48,34,1]{2,0,1:T(8,128)S(1)}, f32[48,34,1]{2,0,1:T(8,128)}, u32[]{:S(2)}) copy-start(f32[48,34,1]{2,0,1:T(8,128)} %copy.56) | copy-start | bytes 19588
  134.0 2.1 %copy-start.15 = (f32[258,258]{1,0:T(8,128)S(1)}, f32[258,258]{1,0:T(8,128)}, u32[]{:S(2)}) copy-start(f32[258,258]{1,0:T(8,128)} %select_maximum_fusion.6) | copy-start | bytes 798772
  134.0 2.1 %copy-start.17 = (f32[1,256]{1,0:T(1,128)S(1)}, f32[1,256]{1,0:T(1,128)}, u32[]{:S(2)}) copy-start(f32[1,256]{1,0:T(1,128)} %copy-done.16) | copy-start | bytes 3076
  134.0 2.1 %copy-start.19 = (f32[1,256]{1,0:T(1,128)S(1)}, f32[1,256]{1,0:T(1,128)}, u32[]{:S(2)}) copy-start(f32[1,256]{1,0:T(1,128)} %copy-done.18) | copy-start | bytes 3076
where the time goes:
time: 139 us; the launch traced here: 137 us
  starting transfers between devices  48 us (35%)
  other arithmetic  42.2 us (30%)
  local copies, waits for them, and re-layouts  37.1 us (27%)
  waiting for transfers between devices  7.54 us (5%)
    add x2, other arithmetic, local(): field = field + diffusivity * stencil_apply(padded)  21.4 us
    ppermute x5, starting transfers between devices, padded_2(): before = lax.ppermute(last, axis, up)  20.3 us
    concatenate x6, other arithmetic, padded_2(): array = jnp.concatenate([before, array, after], axis=dim)  12.9 us
    ppermute x5, starting transfers between devices, padded_2(): after = lax.ppermute(initial, axis, down)  7.91 us
    unnamed x43, local copies, waits for them, and re-layouts  7.73 us
    all_to_all x1, starting transfers between devices, local(): lax.all_to_all(send_gain, 'span', split_axis=0, concat_axis=0, tiled=True)  5.78 us
    concatenate x2, local copies, waits for them, and re-layouts, local(): heated = jnp.concatenate([heated_face[None], die_temp[1:]], axis=0)  5.36 us
    all_to_all x1, starting transfers between devices, local(): lax.all_to_all(send_code, 'span', split_axis=0, concat_axis=0, tiled=True)  5.22 us
  transfers between devices with their start and end apart: 14, of which 3 were waited for; matrix products, arithmetic and copies ran while one was open for 39% of the time, Pallas kernels for 0%

commit v1 on v0

v1 whole, which is shorter than its diff:
```python
import functools

import jax
import jax.numpy as jnp
from jax import lax
from jax.experimental import pallas as pl
from jax.experimental.pallas import tpu as pltpu
from jax.sharding import PartitionSpec as P

SHELL_RATE = 0.15
SHELL_SINK = 0.5
FACE_GAIN = 0.5
MESH = pl.DeviceIdType.MESH
PACK = 128


def split2(x):
    hi = x.astype(jnp.bfloat16)
    lo = (x - hi.astype(jnp.float32)).astype(jnp.bfloat16)
    return hi, lo


def select_dot(select, x):
    hi, lo = split2(x)
    return jnp.dot(select, hi, preferred_element_type=jnp.float32) + jnp.dot(
        select, lo, preferred_element_type=jnp.float32
    )


def kernel(
    n, n_depth, dz, cx,
    code_ref, shell_hbm, gain_hbm, die_hbm, dif_hbm,
    shell_out, die_out,
    v0, v1, dif, shells, gain, faces, flux, partial, arrived,
    xsend, xrecv, hrows_send, hrows, colsend, cols, ucol,
    local_sem, face_send, face_recv, heat_send, heat_recv, send_sem, recv_sem,
):
    s = lax.axis_index("span")
    d = lax.axis_index("depth")
    nb = gain.shape[0]
    f32 = jnp.float32

    def exists(ds, dd):
        return (s + ds >= 0) & (s + ds < n) & (d + dd >= 0) & (d + dd < n_depth)

    def fetch(src, dst, i):
        return pltpu.make_async_copy(src, dst, local_sem.at[i])

    get_face = fetch(die_hbm.at[0], faces.at[s], 0)
    get_shell = fetch(shell_hbm, shells.at[pl.ds(8, nb)], 1)
    get_die = fetch(die_hbm, v0.at[pl.ds(1, dz), pl.ds(8, cx)], 2)
    get_gain = fetch(gain_hbm, gain, 3)
    get_dif = fetch(dif_hbm, dif, 4)
    for c in (get_face, get_shell, get_die, get_gain, get_dif):
        c.start()

    xrecv[...] = jnp.zeros_like(xrecv)
    hrows[...] = jnp.zeros_like(hrows)
    cols[...] = jnp.zeros_like(cols)
    shells[0:8, :] = jnp.zeros((8, shells.shape[1]), f32)
    shells[8 + nb : 16 + nb, :] = jnp.zeros((8, shells.shape[1]), f32)

    barrier = pltpu.get_barrier_semaphore()

    def greet(k, carry):
        pl.semaphore_signal(
            barrier, inc=1, device_id={"span": lax.rem(s + k, n), "depth": d}, device_id_type=MESH
        )
        return carry

    lax.fori_loop(1, n, greet, 0)
    count = jnp.int32(n - 1)
    for ds in (-1, 0, 1):
        for dd in (-1, 1):
            there = exists(ds, dd)
            count = count + there.astype(jnp.int32)

            @pl.when(there)
            def _():
                pl.semaphore_signal(
                    barrier, inc=1, device_id={"span": s + ds, "depth": d + dd}, device_id_type=MESH
                )

    zeros_layer = jnp.zeros(v0.shape[1:], f32)
    for buf in (v0, v1):
        buf[0] = zeros_layer
        buf[dz + 1] = zeros_layer
    pl.semaphore_wait(barrier, count)

    def face_copy(k):
        return pltpu.make_async_remote_copy(
            src_ref=faces.at[s], dst_ref=faces.at[s],
            send_sem=face_send.at[k], recv_sem=face_recv.at[k],
            device_id={"span": lax.rem(s + k, n), "depth": d}, device_id_type=MESH,
        )

    def face_arrival(k):
        return pltpu.make_async_remote_copy(
            src_ref=faces.at[s], dst_ref=faces.at[lax.rem(s + n - k, n)],
            send_sem=face_send.at[k], recv_sem=face_recv.at[k],
            device_id={"span": lax.rem(s + k, n), "depth": d}, device_id_type=MESH,
        )

    def heat_copy(k):
        to = lax.rem(s + k, n)
        return pltpu.make_async_remote_copy(
            src_ref=partial.at[to], dst_ref=arrived.at[k],
            send_sem=heat_send.at[k], recv_sem=heat_recv.at[k],
            device_id={"span": to, "depth": d}, device_id_type=MESH,
        )

    def each_partner(act):
        def step(k, carry):
            act(k)
            return carry

        lax.fori_loop(1, n, step, 0)

    get_face.wait()
    each_partner(lambda k: face_copy(k).start())

    used = [0]

    def message(src, dst, ds, dd):
        i = used[0]
        used[0] += 1
        copy = pltpu.make_async_remote_copy(
            src_ref=src, dst_ref=dst, send_sem=send_sem.at[i], recv_sem=recv_sem.at[i],
            device_id={"span": s + ds, "depth": d + dd}, device_id_type=MESH,
        )
        return copy, ds, dd

    def start(messages):
        for copy, ds, dd in messages:
            pl.when(exists(ds, dd))(copy.start)

    def wait_recv(messages):
        for copy, ds, dd in messages:
            pl.when(exists(-ds, -dd))(copy.wait_recv)

    def wait_send(messages):
        for copy, ds, dd in messages:
            pl.when(exists(ds, dd))(copy.wait_send)

    def column_messages(e):
        out = []
        for side, dd in ((0, -1), (1, 1)):
            src, dst = colsend.at[e, side], cols.at[e, 1 - side]
            out.append(message(src, dst.at[pl.ds(8, cx)], 0, dd))
            out.append(message(src.at[pl.ds(cx - 8, 8)], dst.at[pl.ds(0, 8)], 1, dd))
            out.append(message(src.at[pl.ds(0, 8)], dst.at[pl.ds(8 + cx, 8)], -1, dd))
        return out

    def row_messages(e, at, size):
        return [
            message(xsend.at[e, 0, pl.ds(at, size)], xrecv.at[e, 1, pl.ds(at, size)], -1, 0),
            message(xsend.at[e, 1, pl.ds(at, size)], xrecv.at[e, 0, pl.ds(at, size)], 1, 0),
        ]

    lane = lax.broadcasted_iota(jnp.int32, (cx, PACK), 1)

    def pack(z, layer, left, right):
        at = lane == z
        left = jnp.where(at, pltpu.roll(layer[:, :PACK], z, 1), left)
        right = jnp.where(at, pltpu.roll(layer[:, -PACK:], z + 1, 1), right)
        return left, right

    get_die.wait()

    def pack_two(i, carry):
        left, right = carry
        for j in range(2):
            z = 2 * i + j
            left, right = pack(z, v0[z + 1, 8 : 8 + cx, :], left, right)
        return left, right

    blank = jnp.zeros((cx, PACK), f32)
    left, right = lax.fori_loop(0, dz // 2, pack_two, (blank, blank))
    colsend[0, 0] = left
    colsend[0, 1] = right
    width = v0.shape[2]

    def stage_rows(e, ref):
        xsend[e, 0] = ref[1 : 1 + dz, 8, :]
        xsend[e, 1] = ref[1 : 1 + dz, 7 + cx, :]

    def place_rows(e, ref):
        ref[1 : 1 + dz, 7, :] = xrecv[e, 0]
        ref[1 : 1 + dz, 8 + cx, :] = xrecv[e, 1]

    stage_rows(0, v0)
    get_shell.wait()
    raw = row_messages(0, 0, dz) + column_messages(0)
    raw += [
        message(shells.at[pl.ds(8, 8)], shells.at[pl.ds(8 + nb, 8)], 0, -1),
        message(shells.at[pl.ds(nb, 8)], shells.at[pl.ds(0, 8)], 0, 1),
    ]
    start(raw)

    code_row = code_ref[...]
    code_col = jnp.broadcast_to(code_row, (PACK, nb)).T
    all_rows = n * cx
    step = min(256, all_rows)
    get_gain.wait()
    each_partner(lambda k: face_arrival(k).wait_recv())
    values = jnp.zeros((nb, width), f32)
    lane_rows = lax.broadcasted_iota(jnp.int32, (nb, PACK), 1).astype(f32)
    for at in range(0, all_rows, step):
        pieces = [
            jnp.where(code_col == lane_rows + float(at + j), 1.0, 0.0).astype(jnp.bfloat16)
            for j in range(0, step, PACK)
        ]
        select = jnp.concatenate(pieces, axis=1)
        part = faces[at // cx : (at + step) // cx].reshape(step, width)
        values = values + select_dot(select, part)
    live = jnp.where(code_col >= 0.0, 1.0, 0.0)
    live = jnp.concatenate([live] * (width // PACK), axis=1)
    flux[...] = gain[...] * (shells[8 : 8 + nb, :] - values) * live
    row_ids = lax.broadcasted_iota(jnp.int32, (step, nb), 0).astype(f32)
    hi, lo = split2(flux[...])
    for at in range(0, all_rows, step):
        select = jnp.where(code_row == row_ids + float(at), 1.0, 0.0).astype(jnp.bfloat16)
        heat = jnp.dot(select, hi, preferred_element_type=f32) + jnp.dot(
            select, lo, preferred_element_type=f32
        )
        partial[at // cx : (at + step) // cx] = heat.reshape(step // cx, cx, width)
    each_partner(lambda k: heat_copy(k).start())

    def filter_x(ref, z):
        return ref[z, 7 : 7 + cx, :] + ref[z, 9 : 9 + cx, :] + 2.0 * ref[z, 8 : 8 + cx, :]

    def filter_columns(c):
        p = c[7 : 7 + cx] + c[9 : 9 + cx] + 2.0 * c[8 : 8 + cx]
        return pltpu.roll(p, 1, 1) + pltpu.roll(p, PACK - 1, 1) + 2.0 * p

    def advance(ref, z, before, here, cl, cr):
        after = filter_x(ref, z + 2)
        u = before + after + 2.0 * here
        parts = [u[:, i : i + PACK] for i in range(0, width, PACK)]
        ups = [pltpu.roll(q, 1, 1) for q in parts]
        downs = [pltpu.roll(q, PACK - 1, 1) for q in parts]
        ups = [pltpu.roll(cl, lax.rem(PACK - z, PACK), 1)] + ups
        downs = downs + [pltpu.roll(cr, PACK - 1 - z, 1)]
        mixed = []
        for i, q in enumerate(parts):
            west = jnp.where(lane == 0, ups[i], ups[i + 1])
            east = jnp.where(lane == PACK - 1, downs[i + 1], downs[i])
            mixed.append(west + east + 2.0 * q)
        total = jnp.concatenate(mixed, axis=1)
        v = ref[z + 1, 8 : 8 + cx, :]
        return v + dif[z] * (0.25 * total - 16.0 * v), after

    get_dif.wait()
    wait_recv(raw)
    place_rows(0, v0)
    ucol[0] = filter_columns(cols[0, 0])
    ucol[1] = filter_columns(cols[0, 1])

    def first_two(i, carry):
        before, here, left, right = carry
        for j in range(2):
            z = 2 * i + j
            new, after = advance(v0, z, before, here, ucol[0], ucol[1])
            v1[z + 1, 8 : 8 + cx, :] = new
            left, right = pack(z, new, left, right)
            before, here = here, after
        return before, here, left, right

    _, _, left, right = lax.fori_loop(
        1, dz // 2, first_two, (filter_x(v0, 2), filter_x(v0, 3), blank, blank)
    )
    colsend[2, 0] = left
    colsend[2, 1] = right
    stage_rows(1, v1)
    late_rows = row_messages(1, 8, dz - 8)
    start(late_rows)

    each_partner(lambda k: heat_copy(k).wait_recv())

    def add_up(k, total):
        return total + arrived[k]

    heat_in = lax.fori_loop(1, n, add_up, partial[s])
    face = v0[1, 8 : 8 + cx, :] + FACE_GAIN * heat_in
    v0[1, 8 : 8 + cx, :] = face
    hrows_send[...] = face
    colsend[1, 0] = face[:, :PACK]
    colsend[1, 1] = pltpu.roll(face[:, -PACK:], 1, 1)
    heated = [
        message(hrows_send.at[pl.ds(0, 8)], hrows.at[1], -1, 0),
        message(hrows_send.at[pl.ds(cx - 8, 8)], hrows.at[0], 1, 0),
    ] + column_messages(1)
    start(heated)

    lane_s = lax.broadcasted_iota(jnp.int32, (32, width), 1)
    for r in range(0, nb, 32):
        c = shells[8 + r : 40 + r, :]
        west = jnp.where(lane_s == 0, 0.0, pltpu.roll(c, 1, 1))
        east = jnp.where(lane_s == width - 1, 0.0, pltpu.roll(c, width - 1, 1))
        lap = shells[9 + r : 41 + r, :] + shells[7 + r : 39 + r, :] + east + west - 4.0 * c
        shell_out[r : r + 32, :] = c + SHELL_RATE * lap - SHELL_SINK * flux[r : r + 32, :]

    wait_recv(heated)
    v0[1, 0:8, :] = hrows[0]
    v0[1, 8 + cx : 16 + cx, :] = hrows[1]
    lane_c = lax.broadcasted_iota(jnp.int32, (cols.shape[2], PACK), 1)
    ucol[0] = filter_columns(jnp.where(lane_c == 0, cols[1, 0], cols[0, 0]))
    ucol[1] = filter_columns(jnp.where(lane_c == 0, cols[1, 1], cols[0, 1]))
    before, here = filter_x(v0, 0), filter_x(v0, 1)
    left, right = colsend[2, 0], colsend[2, 1]
    for z in range(2):
        new, after = advance(v0, z, before, here, ucol[0], ucol[1])
        v1[z + 1, 8 : 8 + cx, :] = new
        left, right = pack(z, new, left, right)
        before, here = here, after
    colsend[2, 0] = left
    colsend[2, 1] = right
    xsend[1, 0, 0:8] = v1[1:9, 8, :]
    xsend[1, 1, 0:8] = v1[1:9, 7 + cx, :]
    last = row_messages(1, 0, 8) + column_messages(2)
    start(last)
    wait_recv(late_rows)
    wait_recv(last)
    place_rows(1, v1)
    ucol[0] = filter_columns(cols[2, 0])
    ucol[1] = filter_columns(cols[2, 1])

    def second_two(i, carry):
        before, here = carry
        for j in range(2):
            z = 2 * i + j
            new, after = advance(v1, z, before, here, ucol[0], ucol[1])
            die_out[z] = new
            before, here = here, after
        return before, here

    lax.fori_loop(0, dz // 2, second_two, (filter_x(v1, 0), filter_x(v1, 1)))

    each_partner(lambda k: face_copy(k).wait_send())
    each_partner(lambda k: heat_copy(k).wait_send())
    wait_send(raw + late_rows + heated + last)


def local(n, n_depth, shell_temp, contact_gain, die_temp, diffusivity, routes, tile_rows, closed):
    dz, cx, width = die_temp.shape
    _, nb, _ = shell_temp.shape
    code = jnp.where(closed > 0, routes[:, :, 0] * cx + tile_rows, -1).astype(jnp.float32)
    f32 = jnp.float32
    anywhere = pl.BlockSpec(memory_space=pl.ANY)
    vmem = pl.BlockSpec(memory_space=pltpu.VMEM)
    dma = pltpu.SemaphoreType.DMA
    shell_next, die_next = pl.pallas_call(
        functools.partial(kernel, n, n_depth, dz, cx),
        out_shape=(
            jax.ShapeDtypeStruct((nb, width), f32),
            jax.ShapeDtypeStruct((dz, cx, width), f32),
        ),
        in_specs=[vmem] + [anywhere] * 4,
        out_specs=(vmem, vmem),
        scratch_shapes=[
            pltpu.VMEM((dz + 2, cx + 16, width), f32),
            pltpu.VMEM((dz + 2, cx + 16, width), f32),
            pltpu.VMEM((dz, cx, width), f32),
            pltpu.VMEM((nb + 16, width), f32),
            pltpu.VMEM((nb, width), f32),
            pltpu.VMEM((n, cx, width), f32),
            pltpu.VMEM((nb, width), f32),
            pltpu.VMEM((n, cx, width), f32),
            pltpu.VMEM((n, cx, width), f32),
            pltpu.VMEM((2, 2, dz, width), f32),
            pltpu.VMEM((2, 2, dz, width), f32),
            pltpu.VMEM((cx, width), f32),
            pltpu.VMEM((2, 8, width), f32),
            pltpu.VMEM((3, 2, cx, PACK), f32),
            pltpu.VMEM((3, 2, cx + 16, PACK), f32),
            pltpu.VMEM((2, cx, PACK), f32),
            dma((5,)),
            dma((n,)),
            dma((n,)),
            dma((n,)),
            dma((n,)),
            dma((32,)),
            dma((32,)),
        ],
        compiler_params=pltpu.CompilerParams(
            collective_id=0, has_side_effects=True, vmem_limit_bytes=40 * 1024 * 1024
        ),
        cost_estimate=pl.CostEstimate(flops=20_000_000, bytes_accessed=6_000_000, transcendentals=0),
    )(code, shell_temp[0], contact_gain[0], die_temp, diffusivity)
    return shell_next[None], die_next


def solution(mesh):
    placed = (
        P("span", "depth", None),
        P("span", "depth", None),
        P(None, "span", "depth"),
        P(None, "span", "depth"),
        P("span", "depth", None),
        P("span", "depth"),
        P("span", "depth"),
    )
    return jax.shard_map(
        functools.partial(local, mesh.shape["span"], mesh.shape["depth"]),
        mesh=mesh,
        in_specs=placed,
        out_specs=(P("span", "depth", None), P(None, "span", "depth")),
        check_vma=False,
    )
```

time: 139 us -> 35 us (0.25); the launches traced: 137 us -> 34.8 us
  starting transfers between devices: 48 us -> 0 us
  other arithmetic: 42.2 us -> 0.72 us
  local copies, waits for them, and re-layouts: 37.1 us -> 6.56 us
  Pallas kernels: 0 us -> 26.8 us
  waiting for transfers between devices: 7.54 us -> 0 us
    ppermute x10 -> x0, starting transfers between devices: 28.2 us -> none  [the longest x5 20.3 us: padded_2(): before = lax.ppermute(last, axis, up)]
    pallas_call x0 -> x1, Pallas kernels: none -> 26.8 us  [local(): pl.pallas_call(functools.partial(kernel, n, n_depth, dz, cx), out_shape=(...]
    add x2 -> x0, other arithmetic: 21.4 us -> none  [local(): field = field + diffusivity * stencil_apply(padded)]
    all_to_all x4 -> x0, starting transfers between devices: 19.7 us -> none  [the longest x1 5.78 us: local(): lax.all_to_all(send_gain, 'span', split_axis=0, concat_axis=0, tiled=True)]
    concatenate x7 -> x0, other arithmetic: 13.1 us -> none  [the longest x6 12.9 us: padded_2(): array = jnp.concatenate([before, array, after], axis=dim)]
    concatenate x3 -> x0, local copies, waits for them, and re-layouts: 10.3 us -> none  [the longest x2 5.36 us: local(): heated = jnp.concatenate([heated_face[None], die_temp[1:]], axis=0)]
    scatter x3 -> x0, local copies, waits for them, and re-layouts: 6.24 us -> none  [the longest x1 2.63 us: local(): send_temp = empty_slots.at[position].set(shells)]
    ppermute x6 -> x0, local copies, waits for them, and re-layouts: 4.37 us -> none  [the longest x3 2.67 us: padded_2(): before = lax.ppermute(last, axis, up)]
  transfers between devices with their start and end apart: 14 -> 0, of which waited for: 3 -> 0; matrix products, arithmetic and copies ran while one was open for 39% -> 0% of each run, Pallas kernels for 0% -> 0%
where the time goes in v1:
time: 35 us; the launch traced here: 34.8 us
  Pallas kernels  26.8 us (77%)
  local copies, waits for them, and re-layouts  6.56 us (19%)
  other arithmetic  0.72 us (2%)
  between operations  0.64 us (2%)
    pallas_call x1, Pallas kernels, local(): pl.pallas_call(functools.partial(kernel, n, n_depth, dz, cx), out_shape=(...  26.8 us
    unnamed x10, local copies, waits for them, and re-layouts  6.56 us
    convert_element_type x1, other arithmetic, local(): jnp.where(closed > 0, routes[:, :, 0] * cx + tile_rows, -1)  0.72 us

profile of v1, /device:TPU:1, one launch (start us, length us, event | category | flops | bytes accessed | tf_op | source)
XLA Modules:
  0.0 34.8 jit_solution(7769082919973327257)
XLA Ops:
  0.6 0.7 %fusion.code_ref = f32[1,256]{1,0:T(1,128)S(1)} fusion(s32[1,256]{1,0:T(1,128)} %param.13, s32[1,256]{1,0:T(1,128)} %param.12, s32[1,256,1]{1,2,0:T(1,128)} %param.11), kind=kLoop, calls=%fused_computation.1 | loop fusion | flops 1280 | bytes 4096 | tf_op jit(solution)/shard_map/convert_element_type | solution.py:347
  1.3 0.0 copy-start
  1.4 1.4 %copy-done = f32[48,32,256]{2,1,0:T(8,128)S(1)} copy-done((f32[48,32,256]{2,1,0:T(8,128)S(1)}, f32[48,32,256]{2,1,0:T(8,128)}, u32[]{:S(2)}) %copy-start) | copy-done | bytes 1572888
  2.8 0.0 copy-start.1
  2.8 1.4 %copy-done.1 = f32[48,32,256]{2,1,0:T(8,128)S(1)} copy-done((f32[48,32,256]{2,1,0:T(8,128)S(1)}, f32[48,32,256]{2,1,0:T(8,128)}, u32[]{:S(2)}) %copy-start.1) | copy-done | bytes 1572888
  4.2 0.0 copy-start.2
  4.2 0.9 %copy-done.2 = f32[1,256,256]{2,1,0:T(8,128)S(1)} copy-done((f32[1,256,256]{2,1,0:T(8,128)S(1)}, f32[1,256,256]{2,1,0:T(8,128)}, u32[]{:S(2)}) %copy-start.2) | copy-done | bytes 262168
  5.1 0.0 copy-start.3
  5.1 0.9 %copy-done.3 = f32[1,256,256]{2,1,0:T(8,128)S(1)} copy-done((f32[1,256,256]{2,1,0:T(8,128)S(1)}, f32[1,256,256]{2,1,0:T(8,128)}, u32[]{:S(2)}) %copy-start.3) | copy-done | bytes 262168
  6.1 26.8 %shard_map.86 = (f32[256,256]{1,0:T(8,128)S(1)}, f32[48,32,256]{2,1,0:T(8,128)S(1)}) custom-call(f32[1,256]{1,0:T(1,128)S(1)} %fusion.code_ref, f32[256,256]{1,0:T(8,128)S(1)} %bitcast.8, f32[256,256]{1,0:T(8,128)S(1)} %bitcast.9, f32[48,32,256]{2,1,0:T(8,128)S(1)} %copy-done, f32[48,32,256]{2,1,0:T(8,128)S(1)} %copy-done.1), custom_call_target="tpu_custom_call" | custom-call | flops 20000000 | bytes 6000000 | tf_op jit(solution)/shard_map/pallas_call | solution.py:352
  32.9 0.7 %copy.11 = f32[1,256,256]{2,1,0:T(8,128)} copy(f32[1,256,256]{2,1,0:T(8,128)S(1)} %bitcast.7) | data formatting | bytes 524288
  33.6 1.1 %copy.12 = f32[48,32,256]{2,1,0:T(8,128)} copy(f32[48,32,256]{2,1,0:T(8,128)S(1)} %get-tuple-element.9) | data formatting | bytes 3145728
Async XLA Ops:
  1.3 1.4 %copy-start = (f32[48,32,256]{2,1,0:T(8,128)S(1)}, f32[48,32,256]{2,1,0:T(8,128)}, u32[]{:S(2)}) copy-start(f32[48,32,256]{2,1,0:T(8,128)} %die_hbm.1) | copy-start | bytes 4718596
  2.8 1.4 %copy-start.1 = (f32[48,32,256]{2,1,0:T(8,128)S(1)}, f32[48,32,256]{2,1,0:T(8,128)}, u32[]{:S(2)}) copy-start(f32[48,32,256]{2,1,0:T(8,128)} %dif_hbm.1) | copy-start | bytes 4718596
  4.2 0.9 %copy-start.2 = (f32[1,256,256]{2,1,0:T(8,128)S(1)}, f32[1,256,256]{2,1,0:T(8,128)}, u32[]{:S(2)}) copy-start(f32[1,256,256]{2,1,0:T(8,128)} %param.7) | copy-start | bytes 786436
  5.1 0.9 %copy-start.3 = (f32[1,256,256]{2,1,0:T(8,128)S(1)}, f32[1,256,256]{2,1,0:T(8,128)}, u32[]{:S(2)}) copy-start(f32[1,256,256]{2,1,0:T(8,128)} %param.8) | copy-start | bytes 786436

commit v2 on v1

--- a/solution.py
+++ b/solution.py
@@ -29,10 +29,10 @@
 
 def kernel(
     n, n_depth, dz, cx,
-    code_ref, shell_hbm, gain_hbm, die_hbm, dif_hbm,
+    shell_hbm, gain_hbm, die_hbm, dif_hbm, routes_hbm, tiles_hbm, closed_hbm,
     shell_out, die_out,
     v0, v1, dif, shells, gain, faces, flux, partial, arrived,
-    xsend, xrecv, hrows_send, hrows, colsend, cols, ucol,
+    xsend, xrecv, hrows_send, hrows, lrows_send, lrows, colsend, cols, ucol, codes,
     local_sem, face_send, face_recv, heat_send, heat_recv, send_sem, recv_sem,
 ):
     s = lax.axis_index("span")
@@ -51,11 +51,15 @@
     get_die = fetch(die_hbm, v0.at[pl.ds(1, dz), pl.ds(8, cx)], 2)
     get_gain = fetch(gain_hbm, gain, 3)
     get_dif = fetch(dif_hbm, dif, 4)
-    for c in (get_face, get_shell, get_die, get_gain, get_dif):
+    get_codes = [
+        fetch(ref, codes.at[i], 5 + i) for i, ref in enumerate((routes_hbm, tiles_hbm, closed_hbm))
+    ]
+    for c in [get_face, get_die, get_shell] + get_codes + [get_gain, get_dif]:
         c.start()
 
     xrecv[...] = jnp.zeros_like(xrecv)
     hrows[...] = jnp.zeros_like(hrows)
+    lrows[...] = jnp.zeros_like(lrows)
     cols[...] = jnp.zeros_like(cols)
     shells[0:8, :] = jnp.zeros((8, shells.shape[1]), f32)
     shells[8 + nb : 16 + nb, :] = jnp.zeros((8, shells.shape[1]), f32)
@@ -85,6 +89,8 @@
     for buf in (v0, v1):
         buf[0] = zeros_layer
         buf[dz + 1] = zeros_layer
+    v1[1] = zeros_layer
+    v1[2] = zeros_layer
     pl.semaphore_wait(barrier, count)
 
     def face_copy(k):
@@ -151,10 +157,10 @@
             out.append(message(src.at[pl.ds(0, 8)], dst.at[pl.ds(8 + cx, 8)], -1, dd))
         return out
 
-    def row_messages(e, at, size):
+    def row_messages(e):
         return [
-            message(xsend.at[e, 0, pl.ds(at, size)], xrecv.at[e, 1, pl.ds(at, size)], -1, 0),
-            message(xsend.at[e, 1, pl.ds(at, size)], xrecv.at[e, 0, pl.ds(at, size)], 1, 0),
+            message(xsend.at[e, 0], xrecv.at[e, 1], -1, 0),
+            message(xsend.at[e, 1], xrecv.at[e, 0], 1, 0),
         ]
 
     lane = lax.broadcasted_iota(jnp.int32, (cx, PACK), 1)
@@ -167,15 +173,15 @@
 
     get_die.wait()
 
-    def pack_two(i, carry):
+    def pack_some(i, carry):
         left, right = carry
-        for j in range(2):
-            z = 2 * i + j
+        for j in range(4):
+            z = 4 * i + j
             left, right = pack(z, v0[z + 1, 8 : 8 + cx, :], left, right)
         return left, right
 
     blank = jnp.zeros((cx, PACK), f32)
-    left, right = lax.fori_loop(0, dz // 2, pack_two, (blank, blank))
+    left, right = lax.fori_loop(0, dz // 4, pack_some, (blank, blank))
     colsend[0, 0] = left
     colsend[0, 1] = right
     width = v0.shape[2]
@@ -190,14 +196,16 @@
 
     stage_rows(0, v0)
     get_shell.wait()
-    raw = row_messages(0, 0, dz) + column_messages(0)
+    raw = row_messages(0) + column_messages(0)
     raw += [
         message(shells.at[pl.ds(8, 8)], shells.at[pl.ds(8 + nb, 8)], 0, -1),
         message(shells.at[pl.ds(nb, 8)], shells.at[pl.ds(0, 8)], 0, 1),
     ]
     start(raw)
 
-    code_row = code_ref[...]
+    for c in get_codes:
+        c.wait()
+    code_row = jnp.where(codes[2] > 0, codes[0] * cx + codes[1], -1).astype(f32)
     code_col = jnp.broadcast_to(code_row, (PACK, nb)).T
     all_rows = n * cx
     step = min(256, all_rows)
@@ -272,8 +280,8 @@
     colsend[2, 0] = left
     colsend[2, 1] = right
     stage_rows(1, v1)
-    late_rows = row_messages(1, 8, dz - 8)
-    start(late_rows)
+    early = row_messages(1) + column_messages(2)
+    start(early)
 
     each_partner(lambda k: heat_copy(k).wait_recv())
 
@@ -300,6 +308,23 @@
         lap = shells[9 + r : 41 + r, :] + shells[7 + r : 39 + r, :] + east + west - 4.0 * c
         shell_out[r : r + 32, :] = c + SHELL_RATE * lap - SHELL_SINK * flux[r : r + 32, :]
 
+    wait_recv(early)
+    place_rows(1, v1)
+    ucol[2] = filter_columns(cols[2, 0])
+    ucol[3] = filter_columns(cols[2, 1])
+
+    def second_three(i, carry):
+        before, here = carry
+        for j in range(3):
+            z = 3 * i + j
+            new, after = advance(v1, z, before, here, ucol[2], ucol[3])
+            die_out[z] = new
+            before, here = here, after
+        return before, here
+
+    middle = dz // 6
+    state = lax.fori_loop(1, middle, second_three, (filter_x(v1, 3), filter_x(v1, 4)))
+
     wait_recv(heated)
     v0[1, 0:8, :] = hrows[0]
     v0[1, 8 + cx : 16 + cx, :] = hrows[1]
@@ -307,46 +332,46 @@
     ucol[0] = filter_columns(jnp.where(lane_c == 0, cols[1, 0], cols[0, 0]))
     ucol[1] = filter_columns(jnp.where(lane_c == 0, cols[1, 1], cols[0, 1]))
     before, here = filter_x(v0, 0), filter_x(v0, 1)
-    left, right = colsend[2, 0], colsend[2, 1]
+    left, right = blank, blank
     for z in range(2):
         new, after = advance(v0, z, before, here, ucol[0], ucol[1])
         v1[z + 1, 8 : 8 + cx, :] = new
+        lrows_send[0, z : z + 1, :] = new[0:1]
+        lrows_send[1, z : z + 1, :] = new[cx - 1 : cx]
         left, right = pack(z, new, left, right)
         before, here = here, after
-    colsend[2, 0] = left
-    colsend[2, 1] = right
-    xsend[1, 0, 0:8] = v1[1:9, 8, :]
-    xsend[1, 1, 0:8] = v1[1:9, 7 + cx, :]
-    last = row_messages(1, 0, 8) + column_messages(2)
+    colsend[3, 0] = left
+    colsend[3, 1] = right
+    last = [
+        message(lrows_send.at[0], lrows.at[1], -1, 0),
+        message(lrows_send.at[1], lrows.at[0], 1, 0),
+    ] + column_messages(3)
     start(last)
-    wait_recv(late_rows)
+
+    lax.fori_loop(middle, dz // 3, second_three, state)
+
     wait_recv(last)
-    place_rows(1, v1)
-    ucol[0] = filter_columns(cols[2, 0])
-    ucol[1] = filter_columns(cols[2, 1])
-
-    def second_two(i, carry):
-        before, here = carry
-        for j in range(2):
-            z = 2 * i + j
-            new, after = advance(v1, z, before, here, ucol[0], ucol[1])
-            die_out[z] = new
-            before, here = here, after
-        return before, here
-
-    lax.fori_loop(0, dz // 2, second_two, (filter_x(v1, 0), filter_x(v1, 1)))
+    for z in range(2):
+        v1[z + 1, 7:8, :] = lrows[0, z : z + 1, :]
+        v1[z + 1, 8 + cx : 9 + cx, :] = lrows[1, z : z + 1, :]
+    ucol[0] = filter_columns(jnp.where(lane_c < 2, cols[3, 0], cols[2, 0]))
+    ucol[1] = filter_columns(jnp.where(lane_c < 2, cols[3, 1], cols[2, 1]))
+    before, here = filter_x(v1, 0), filter_x(v1, 1)
+    for z in range(3):
+        new, after = advance(v1, z, before, here, ucol[0], ucol[1])
+        die_out[z] = new
+        before, here = here, after
 
     each_partner(lambda k: face_copy(k).wait_send())
     each_partner(lambda k: heat_copy(k).wait_send())
-    wait_send(raw + late_rows + heated + last)
+    wait_send(raw + early + heated + last)
 
 
 def local(n, n_depth, shell_temp, contact_gain, die_temp, diffusivity, routes, tile_rows, closed):
     dz, cx, width = die_temp.shape
     _, nb, _ = shell_temp.shape
-    code = jnp.where(closed > 0, routes[:, :, 0] * cx + tile_rows, -1).astype(jnp.float32)
     f32 = jnp.float32
-    anywhere = pl.BlockSpec(memory_space=pl.ANY)
+    hbm = pl.BlockSpec(memory_space=pltpu.HBM)
     vmem = pl.BlockSpec(memory_space=pltpu.VMEM)
     dma = pltpu.SemaphoreType.DMA
     shell_next, die_next = pl.pallas_call(
@@ -355,7 +380,7 @@
             jax.ShapeDtypeStruct((nb, width), f32),
             jax.ShapeDtypeStruct((dz, cx, width), f32),
         ),
-        in_specs=[vmem] + [anywhere] * 4,
+        in_specs=[hbm] * 7,
         out_specs=(vmem, vmem),
         scratch_shapes=[
             pltpu.VMEM((dz + 2, cx + 16, width), f32),
@@ -371,22 +396,33 @@
             pltpu.VMEM((2, 2, dz, width), f32),
             pltpu.VMEM((cx, width), f32),
             pltpu.VMEM((2, 8, width), f32),
-            pltpu.VMEM((3, 2, cx, PACK), f32),
-            pltpu.VMEM((3, 2, cx + 16, PACK), f32),
-            pltpu.VMEM((2, cx, PACK), f32),
-            dma((5,)),
+            pltpu.VMEM((2, 8, width), f32),
+            pltpu.VMEM((2, 8, width), f32),
+            pltpu.VMEM((4, 2, cx, PACK), f32),
+            pltpu.VMEM((4, 2, cx + 16, PACK), f32),
+            pltpu.VMEM((4, cx, PACK), f32),
+            pltpu.VMEM((3, 1, nb), jnp.int32),
+            dma((8,)),
             dma((n,)),
             dma((n,)),
             dma((n,)),
             dma((n,)),
-            dma((32,)),
-            dma((32,)),
+            dma((40,)),
+            dma((40,)),
         ],
         compiler_params=pltpu.CompilerParams(
             collective_id=0, has_side_effects=True, vmem_limit_bytes=40 * 1024 * 1024
         ),
         cost_estimate=pl.CostEstimate(flops=20_000_000, bytes_accessed=6_000_000, transcendentals=0),
-    )(code, shell_temp[0], contact_gain[0], die_temp, diffusivity)
+    )(
+        *(
+            pltpu.with_memory_space_constraint(x, pltpu.HBM)
+            for x in (
+                shell_temp[0], contact_gain[0], die_temp, diffusivity,
+                routes[:, :, 0], tile_rows, closed,
+            )
+        )
+    )
     return shell_next[None], die_next
 
 

time: 35 us -> 27.5 us (0.79)
  local copies, waits for them, and re-layouts: 6.56 us -> 1.85 us
  Pallas kernels: 26.8 us -> 24.9 us
  other arithmetic: 0.72 us -> 0 us
    unnamed x10 -> x2, local copies, waits for them, and re-layouts: 6.56 us -> 1.85 us
    pallas_call x1, Pallas kernels: 26.8 us -> 24.9 us  [local(): pl.pallas_call(functools.partial(kernel, n, n_depth, dz, cx), out_shape=(...]
    convert_element_type x1 -> x0, other arithmetic: 0.72 us -> none  [local(): jnp.where(closed > 0, routes[:, :, 0] * cx + tile_rows, -1)]
where the time goes in v2:
time: 27.5 us; the launch traced here: 27.4 us
  Pallas kernels  24.9 us (91%)
  local copies, waits for them, and re-layouts  1.85 us (7%)
  between operations  0.64 us (2%)
    pallas_call x1, Pallas kernels, local(): pl.pallas_call(functools.partial(kernel, n, n_depth, dz, cx), out_shape=(...  24.9 us
    unnamed x2, local copies, waits for them, and re-layouts  1.85 us

profile of v2, /device:TPU:1, one launch (start us, length us, event | category | flops | bytes accessed | tf_op | source)
XLA Modules:
  0.0 27.4 jit_solution(7134512955898078854)
XLA Ops:
  0.6 24.9 %shard_map.86 = (f32[256,256]{1,0:T(8,128)S(1)}, f32[48,32,256]{2,1,0:T(8,128)S(1)}) custom-call(f32[256,256]{1,0:T(8,128)} %bitcast.5, f32[256,256]{1,0:T(8,128)} %bitcast.6, f32[48,32,256]{2,1,0:T(8,128)} %die_hbm.1, f32[48,32,256]{2,1,0:T(8,128)} %dif_hbm.1, s32[1,256]{1,0:T(1,128)} %bitcast.7, s32[1,256]{1,0:T(1,128)} %tiles_hbm.1, s32[1,256]{1,0:T(1,128)} %closed_hbm.1), custom_call_target="tpu_custom_call" | custom-call | flops 20000000 | bytes 6000000 | tf_op jit(solution)/shard_map/pallas_call | solution.py:377
  25.5 0.7 %copy.11 = f32[1,256,256]{2,1,0:T(8,128)} copy(f32[1,256,256]{2,1,0:T(8,128)S(1)} %bitcast.4) | data formatting | bytes 524288
  26.2 1.1 %copy.12 = f32[48,32,256]{2,1,0:T(8,128)} copy(f32[48,32,256]{2,1,0:T(8,128)S(1)} %get-tuple-element.9) | data formatting | bytes 3145728

commit v3 on v2

--- a/solution.py
+++ b/solution.py
@@ -32,7 +32,7 @@
     shell_hbm, gain_hbm, die_hbm, dif_hbm, routes_hbm, tiles_hbm, closed_hbm,
     shell_out, die_out,
     v0, v1, dif, shells, gain, faces, flux, partial, arrived,
-    xsend, xrecv, hrows_send, hrows, lrows_send, lrows, colsend, cols, ucol, codes,
+    xsend, xrecv, hrows_send, hrows, lrows_send, lrows, colsend, cols, ucol, codes, pick, put,
     local_sem, face_send, face_recv, heat_send, heat_recv, send_sem, recv_sem,
 ):
     s = lax.axis_index("span")
@@ -209,25 +209,28 @@
     code_col = jnp.broadcast_to(code_row, (PACK, nb)).T
     all_rows = n * cx
     step = min(256, all_rows)
+    lane_rows = lax.broadcasted_iota(jnp.int32, (nb, PACK), 1).astype(f32)
+    row_ids = lax.broadcasted_iota(jnp.int32, (step, nb), 0).astype(f32)
+    for at in range(0, all_rows, step):
+        for j in range(at, at + step, PACK):
+            pick[:, j : j + PACK] = jnp.where(code_col == lane_rows + float(j), 1.0, 0.0).astype(
+                jnp.bfloat16
+            )
+        put[at : at + step, :] = jnp.where(code_row == row_ids + float(at), 1.0, 0.0).astype(
+            jnp.bfloat16
+        )
     get_gain.wait()
     each_partner(lambda k: face_arrival(k).wait_recv())
     values = jnp.zeros((nb, width), f32)
-    lane_rows = lax.broadcasted_iota(jnp.int32, (nb, PACK), 1).astype(f32)
     for at in range(0, all_rows, step):
-        pieces = [
-            jnp.where(code_col == lane_rows + float(at + j), 1.0, 0.0).astype(jnp.bfloat16)
-            for j in range(0, step, PACK)
-        ]
-        select = jnp.concatenate(pieces, axis=1)
         part = faces[at // cx : (at + step) // cx].reshape(step, width)
-        values = values + select_dot(select, part)
+        values = values + select_dot(pick[:, at : at + step], part)
     live = jnp.where(code_col >= 0.0, 1.0, 0.0)
     live = jnp.concatenate([live] * (width // PACK), axis=1)
     flux[...] = gain[...] * (shells[8 : 8 + nb, :] - values) * live
-    row_ids = lax.broadcasted_iota(jnp.int32, (step, nb), 0).astype(f32)
     hi, lo = split2(flux[...])
     for at in range(0, all_rows, step):
-        select = jnp.where(code_row == row_ids + float(at), 1.0, 0.0).astype(jnp.bfloat16)
+        select = put[at : at + step, :]
         heat = jnp.dot(select, hi, preferred_element_type=f32) + jnp.dot(
             select, lo, preferred_element_type=f32
         )
@@ -264,24 +267,30 @@
     ucol[0] = filter_columns(cols[0, 0])
     ucol[1] = filter_columns(cols[0, 1])
 
-    def first_two(i, carry):
+    def first(z, carry, count):
         before, here, left, right = carry
-        for j in range(2):
-            z = 2 * i + j
-            new, after = advance(v0, z, before, here, ucol[0], ucol[1])
-            v1[z + 1, 8 : 8 + cx, :] = new
-            left, right = pack(z, new, left, right)
+        for j in range(count):
+            new, after = advance(v0, z + j, before, here, ucol[0], ucol[1])
+            v1[z + j + 1, 8 : 8 + cx, :] = new
+            left, right = pack(z + j, new, left, right)
             before, here = here, after
         return before, here, left, right
 
-    _, _, left, right = lax.fori_loop(
-        1, dz // 2, first_two, (filter_x(v0, 2), filter_x(v0, 3), blank, blank)
-    )
+    state = first(2, (filter_x(v0, 2), filter_x(v0, 3), blank, blank), 2)
+    _, _, left, right = lax.fori_loop(1, dz // 4, lambda i, c: first(4 * i, c, 4), state)
     colsend[2, 0] = left
     colsend[2, 1] = right
     stage_rows(1, v1)
     early = row_messages(1) + column_messages(2)
     start(early)
+
+    lane_s = lax.broadcasted_iota(jnp.int32, (32, width), 1)
+    for r in range(0, nb, 32):
+        c = shells[8 + r : 40 + r, :]
+        west = jnp.where(lane_s == 0, 0.0, pltpu.roll(c, 1, 1))
+        east = jnp.where(lane_s == width - 1, 0.0, pltpu.roll(c, width - 1, 1))
+        lap = shells[9 + r : 41 + r, :] + shells[7 + r : 39 + r, :] + east + west - 4.0 * c
+        shell_out[r : r + 32, :] = c + SHELL_RATE * lap - SHELL_SINK * flux[r : r + 32, :]
 
     each_partner(lambda k: heat_copy(k).wait_recv())
 
@@ -300,30 +309,22 @@
     ] + column_messages(1)
     start(heated)
 
-    lane_s = lax.broadcasted_iota(jnp.int32, (32, width), 1)
-    for r in range(0, nb, 32):
-        c = shells[8 + r : 40 + r, :]
-        west = jnp.where(lane_s == 0, 0.0, pltpu.roll(c, 1, 1))
-        east = jnp.where(lane_s == width - 1, 0.0, pltpu.roll(c, width - 1, 1))
-        lap = shells[9 + r : 41 + r, :] + shells[7 + r : 39 + r, :] + east + west - 4.0 * c
-        shell_out[r : r + 32, :] = c + SHELL_RATE * lap - SHELL_SINK * flux[r : r + 32, :]
-
     wait_recv(early)
     place_rows(1, v1)
     ucol[2] = filter_columns(cols[2, 0])
     ucol[3] = filter_columns(cols[2, 1])
 
-    def second_three(i, carry):
+    def second(i, carry):
         before, here = carry
-        for j in range(3):
-            z = 3 * i + j
+        for j in range(5):
+            z = 5 * i + j + 3
             new, after = advance(v1, z, before, here, ucol[2], ucol[3])
             die_out[z] = new
             before, here = here, after
         return before, here
 
-    middle = dz // 6
-    state = lax.fori_loop(1, middle, second_three, (filter_x(v1, 3), filter_x(v1, 4)))
+    turns = (dz - 3) // 5
+    state = lax.fori_loop(0, turns // 2, second, (filter_x(v1, 3), filter_x(v1, 4)))
 
     wait_recv(heated)
     v0[1, 0:8, :] = hrows[0]
@@ -348,7 +349,7 @@
     ] + column_messages(3)
     start(last)
 
-    lax.fori_loop(middle, dz // 3, second_three, state)
+    lax.fori_loop(turns // 2, turns, second, state)
 
     wait_recv(last)
     for z in range(2):
@@ -365,6 +366,19 @@
     each_partner(lambda k: face_copy(k).wait_send())
     each_partner(lambda k: heat_copy(k).wait_send())
     wait_send(raw + early + heated + last)
+
+
+def store(shell_in, die_in, shell_hbm, die_hbm, sems):
+    dz = die_in.shape[0]
+    part = dz // 4
+    copies = [pltpu.make_async_copy(shell_in, shell_hbm, sems.at[4])]
+    for i in range(4):
+        span = pl.ds(i * part, part)
+        copies.append(pltpu.make_async_copy(die_in.at[span], die_hbm.at[span], sems.at[i]))
+    for c in copies:
+        c.start()
+    for c in copies:
+        c.wait()
 
 
 def local(n, n_depth, shell_temp, contact_gain, die_temp, diffusivity, routes, tile_rows, closed):
@@ -402,6 +416,8 @@
             pltpu.VMEM((4, 2, cx + 16, PACK), f32),
             pltpu.VMEM((4, cx, PACK), f32),
             pltpu.VMEM((3, 1, nb), jnp.int32),
+            pltpu.VMEM((nb, n * cx), jnp.bfloat16),
+            pltpu.VMEM((n * cx, nb), jnp.bfloat16),
             dma((8,)),
             dma((n,)),
             dma((n,)),
@@ -423,6 +439,17 @@
             )
         )
     )
+    anywhere = pl.BlockSpec(memory_space=pl.ANY)
+    shell_next, die_next = pl.pallas_call(
+        store,
+        out_shape=(
+            jax.ShapeDtypeStruct((nb, width), f32),
+            jax.ShapeDtypeStruct((dz, cx, width), f32),
+        ),
+        in_specs=[vmem, vmem],
+        out_specs=(anywhere, anywhere),
+        scratch_shapes=[dma((5,))],
+    )(shell_next, die_next)
     return shell_next[None], die_next
 
 

time: 27.5 us -> 29 us (1.055)
  Pallas kernels: 24.9 us -> 26.3 us
    pallas_call x0 -> x1, Pallas kernels: none -> 2.76 us  [local(): pl.pallas_call(store, out_shape=(jax.ShapeDtypeStruct((nb, width), f32),...]
    pallas_call x1, Pallas kernels: 24.9 us -> 23.6 us  [local(): pl.pallas_call(functools.partial(kernel, n, n_depth, dz, cx), out_shape=(...]
    unnamed x2 -> x4, local copies, waits for them, and re-layouts: 1.85 us -> 1.87 us
where the time goes in v3:
time: 29 us; the launch traced here: 28.8 us
  Pallas kernels  26.3 us (91%)
  local copies, waits for them, and re-layouts  1.87 us (6%)
  between operations  0.65 us (2%)
    pallas_call x1, Pallas kernels, local(): pl.pallas_call(functools.partial(kernel, n, n_depth, dz, cx), out_shape=(...  23.6 us
    pallas_call x1, Pallas kernels, local(): pl.pallas_call(store, out_shape=(jax.ShapeDtypeStruct((nb, width), f32),...  2.76 us
    unnamed x4, local copies, waits for them, and re-layouts  1.87 us

profile of v3, /device:TPU:1, one launch (start us, length us, event | category | flops | bytes accessed | tf_op | source)
XLA Modules:
  0.0 28.8 jit_solution(16207967554810193150)
XLA Ops:
  0.6 23.6 %shard_map.86 = (f32[256,256]{1,0:T(8,128)S(1)}, f32[48,32,256]{2,1,0:T(8,128)S(1)}) custom-call(f32[256,256]{1,0:T(8,128)} %bitcast.4, f32[256,256]{1,0:T(8,128)} %bitcast.5, f32[48,32,256]{2,1,0:T(8,128)} %die_hbm.1, f32[48,32,256]{2,1,0:T(8,128)} %dif_hbm.1, s32[1,256]{1,0:T(1,128)} %bitcast.6, s32[1,256]{1,0:T(1,128)} %tiles_hbm.1, s32[1,256]{1,0:T(1,128)} %closed_hbm.1), custom_call_target="tpu_custom_call" | custom-call | flops 20000000 | bytes 6000000 | tf_op jit(solution)/shard_map/pallas_call | solution.py:391
  24.2 0.0 copy-start
  24.2 1.2 %copy-done = f32[48,32,256]{2,1,0:T(8,128)} copy-done((f32[48,32,256]{2,1,0:T(8,128)}, f32[48,32,256]{2,1,0:T(8,128)S(1)}, u32[]{:S(2)}) %copy-start) | copy-done | bytes 1572888
  25.4 0.0 copy-start.1
  25.4 0.7 %copy-done.1 = f32[256,256]{1,0:T(8,128)} copy-done((f32[256,256]{1,0:T(8,128)}, f32[256,256]{1,0:T(8,128)S(1)}, u32[]{:S(2)}) %copy-start.1) | copy-done | bytes 262168
  26.1 2.8 %shard_map.87 = (f32[256,256]{1,0:T(8,128)}, f32[48,32,256]{2,1,0:T(8,128)}) custom-call(f32[256,256]{1,0:T(8,128)} %copy-done.1, f32[48,32,256]{2,1,0:T(8,128)} %copy-done), custom_call_target="tpu_custom_call" | custom-call | tf_op jit(solution)/shard_map/pallas_call | solution.py:443
Async XLA Ops:
  24.2 1.2 %copy-start = (f32[48,32,256]{2,1,0:T(8,128)}, f32[48,32,256]{2,1,0:T(8,128)S(1)}, u32[]{:S(2)}) copy-start(f32[48,32,256]{2,1,0:T(8,128)S(1)} %get-tuple-element.7.die_in) | copy-start | bytes 4718596
  25.4 0.7 %copy-start.1 = (f32[256,256]{1,0:T(8,128)}, f32[256,256]{1,0:T(8,128)S(1)}, u32[]{:S(2)}) copy-start(f32[256,256]{1,0:T(8,128)S(1)} %get-tuple-element.6.shell_in) | copy-start | bytes 786436

commit v4 on v3

--- a/solution.py
+++ b/solution.py
@@ -175,13 +175,13 @@
 
     def pack_some(i, carry):
         left, right = carry
-        for j in range(4):
-            z = 4 * i + j
+        for j in range(8):
+            z = 8 * i + j
             left, right = pack(z, v0[z + 1, 8 : 8 + cx, :], left, right)
         return left, right
 
     blank = jnp.zeros((cx, PACK), f32)
-    left, right = lax.fori_loop(0, dz // 4, pack_some, (blank, blank))
+    left, right = lax.fori_loop(0, dz // 8, pack_some, (blank, blank))
     colsend[0, 0] = left
     colsend[0, 1] = right
     width = v0.shape[2]
@@ -277,7 +277,7 @@
         return before, here, left, right
 
     state = first(2, (filter_x(v0, 2), filter_x(v0, 3), blank, blank), 2)
-    _, _, left, right = lax.fori_loop(1, dz // 4, lambda i, c: first(4 * i, c, 4), state)
+    _, _, left, right = lax.fori_loop(0, (dz - 4) // 11, lambda i, c: first(11 * i + 4, c, 11), state)
     colsend[2, 0] = left
     colsend[2, 1] = right
     stage_rows(1, v1)
@@ -316,14 +316,14 @@
 
     def second(i, carry):
         before, here = carry
-        for j in range(5):
-            z = 5 * i + j + 3
+        for j in range(9):
+            z = 9 * i + j + 3
             new, after = advance(v1, z, before, here, ucol[2], ucol[3])
             die_out[z] = new
             before, here = here, after
         return before, here
 
-    turns = (dz - 3) // 5
+    turns = (dz - 3) // 9
     state = lax.fori_loop(0, turns // 2, second, (filter_x(v1, 3), filter_x(v1, 4)))
 
     wait_recv(heated)
@@ -366,19 +366,6 @@
     each_partner(lambda k: face_copy(k).wait_send())
     each_partner(lambda k: heat_copy(k).wait_send())
     wait_send(raw + early + heated + last)
-
-
-def store(shell_in, die_in, shell_hbm, die_hbm, sems):
-    dz = die_in.shape[0]
-    part = dz // 4
-    copies = [pltpu.make_async_copy(shell_in, shell_hbm, sems.at[4])]
-    for i in range(4):
-        span = pl.ds(i * part, part)
-        copies.append(pltpu.make_async_copy(die_in.at[span], die_hbm.at[span], sems.at[i]))
-    for c in copies:
-        c.start()
-    for c in copies:
-        c.wait()
 
 
 def local(n, n_depth, shell_temp, contact_gain, die_temp, diffusivity, routes, tile_rows, closed):
@@ -439,17 +426,6 @@
             )
         )
     )
-    anywhere = pl.BlockSpec(memory_space=pl.ANY)
-    shell_next, die_next = pl.pallas_call(
-        store,
-        out_shape=(
-            jax.ShapeDtypeStruct((nb, width), f32),
-            jax.ShapeDtypeStruct((dz, cx, width), f32),
-        ),
-        in_specs=[vmem, vmem],
-        out_specs=(anywhere, anywhere),
-        scratch_shapes=[dma((5,))],
-    )(shell_next, die_next)
     return shell_next[None], die_next
 
 

time: 29 us -> 26 us (0.90)
  Pallas kernels: 26.3 us -> 23.4 us
    pallas_call x1 -> x0, Pallas kernels: 2.76 us -> none  [local(): pl.pallas_call(store, out_shape=(jax.ShapeDtypeStruct((nb, width), f32),...]
    unnamed x4 -> x2, local copies, waits for them, and re-layouts: 1.87 us -> 1.85 us
where the time goes in v4:
time: 26 us; the launch traced here: 25.9 us
  Pallas kernels  23.4 us (90%)
  local copies, waits for them, and re-layouts  1.85 us (7%)
  between operations  0.64 us (2%)
    pallas_call x1, Pallas kernels, local(): pl.pallas_call(functools.partial(kernel, n, n_depth, dz, cx), out_shape=(...  23.4 us
    unnamed x2, local copies, waits for them, and re-layouts  1.85 us

profile of v4, /device:TPU:1, one launch (start us, length us, event | category | flops | bytes accessed | tf_op | source)
XLA Modules:
  0.0 25.9 jit_solution(11525327166407753694)
XLA Ops:
  0.6 23.4 %shard_map.86 = (f32[256,256]{1,0:T(8,128)S(1)}, f32[48,32,256]{2,1,0:T(8,128)S(1)}) custom-call(f32[256,256]{1,0:T(8,128)} %bitcast.5, f32[256,256]{1,0:T(8,128)} %bitcast.6, f32[48,32,256]{2,1,0:T(8,128)} %die_hbm.1, f32[48,32,256]{2,1,0:T(8,128)} %dif_hbm.1, s32[1,256]{1,0:T(1,128)} %bitcast.7, s32[1,256]{1,0:T(1,128)} %tiles_hbm.1, s32[1,256]{1,0:T(1,128)} %closed_hbm.1), custom_call_target="tpu_custom_call" | custom-call | flops 20000000 | bytes 6000000 | tf_op jit(solution)/shard_map/pallas_call | solution.py:378
  24.0 0.7 %copy.11 = f32[1,256,256]{2,1,0:T(8,128)} copy(f32[1,256,256]{2,1,0:T(8,128)S(1)} %bitcast.4) | data formatting | bytes 524288
  24.7 1.1 %copy.12 = f32[48,32,256]{2,1,0:T(8,128)} copy(f32[48,32,256]{2,1,0:T(8,128)S(1)} %get-tuple-element.9) | data formatting | bytes 3145728

commit v5 on v4

--- a/solution.py
+++ b/solution.py
@@ -284,14 +284,6 @@
     early = row_messages(1) + column_messages(2)
     start(early)
 
-    lane_s = lax.broadcasted_iota(jnp.int32, (32, width), 1)
-    for r in range(0, nb, 32):
-        c = shells[8 + r : 40 + r, :]
-        west = jnp.where(lane_s == 0, 0.0, pltpu.roll(c, 1, 1))
-        east = jnp.where(lane_s == width - 1, 0.0, pltpu.roll(c, width - 1, 1))
-        lap = shells[9 + r : 41 + r, :] + shells[7 + r : 39 + r, :] + east + west - 4.0 * c
-        shell_out[r : r + 32, :] = c + SHELL_RATE * lap - SHELL_SINK * flux[r : r + 32, :]
-
     each_partner(lambda k: heat_copy(k).wait_recv())
 
     def add_up(k, total):
@@ -308,6 +300,14 @@
         message(hrows_send.at[pl.ds(cx - 8, 8)], hrows.at[0], 1, 0),
     ] + column_messages(1)
     start(heated)
+
+    lane_s = lax.broadcasted_iota(jnp.int32, (32, width), 1)
+    for r in range(0, nb, 32):
+        c = shells[8 + r : 40 + r, :]
+        west = jnp.where(lane_s == 0, 0.0, pltpu.roll(c, 1, 1))
+        east = jnp.where(lane_s == width - 1, 0.0, pltpu.roll(c, width - 1, 1))
+        lap = shells[9 + r : 41 + r, :] + shells[7 + r : 39 + r, :] + east + west - 4.0 * c
+        shell_out[r : r + 32, :] = c + SHELL_RATE * lap - SHELL_SINK * flux[r : r + 32, :]
 
     wait_recv(early)
     place_rows(1, v1)

time: 26 us -> 26 us (level)
  no operation moved by 1% of the time
where the time goes in v5:
time: 26 us; the launch traced here: 25.9 us
  Pallas kernels  23.4 us (90%)
  local copies, waits for them, and re-layouts  1.85 us (7%)
  between operations  0.64 us (2%)
    pallas_call x1, Pallas kernels, local(): pl.pallas_call(functools.partial(kernel, n, n_depth, dz, cx), out_shape=(...  23.4 us
    unnamed x2, local copies, waits for them, and re-layouts  1.85 us

profile of v5, /device:TPU:1, one launch (start us, length us, event | category | flops | bytes accessed | tf_op | source)
XLA Modules:
  0.0 25.9 jit_solution(4135596824582184699)
XLA Ops:
  0.6 23.4 %shard_map.86 = (f32[256,256]{1,0:T(8,128)S(1)}, f32[48,32,256]{2,1,0:T(8,128)S(1)}) custom-call(f32[256,256]{1,0:T(8,128)} %bitcast.5, f32[256,256]{1,0:T(8,128)} %bitcast.6, f32[48,32,256]{2,1,0:T(8,128)} %die_hbm.1, f32[48,32,256]{2,1,0:T(8,128)} %dif_hbm.1, s32[1,256]{1,0:T(1,128)} %bitcast.7, s32[1,256]{1,0:T(1,128)} %tiles_hbm.1, s32[1,256]{1,0:T(1,128)} %closed_hbm.1), custom_call_target="tpu_custom_call" | custom-call | flops 20000000 | bytes 6000000 | tf_op jit(solution)/shard_map/pallas_call | solution.py:378
  24.0 0.7 %copy.11 = f32[1,256,256]{2,1,0:T(8,128)} copy(f32[1,256,256]{2,1,0:T(8,128)S(1)} %bitcast.4) | data formatting | bytes 524288
  24.7 1.1 %copy.12 = f32[48,32,256]{2,1,0:T(8,128)} copy(f32[48,32,256]{2,1,0:T(8,128)S(1)} %get-tuple-element.9) | data formatting | bytes 3145728
